TPU v7x, 32 devices: a whole 2x2x4 slice. The times are simulated.
32 devices in a mesh: own: 4 (over y, x), br: 8 (over z, core).
Axes of the slice: x: 2, y: 2, z: 4, core: 2. Of those that a mesh axis runs over, the one named last changes fastest.
Arguments:
- queries: bfloat16 [32, 256, 5120], P('br', None, 'own'), may hold values from -6 to 6
- branch_keys: bfloat16 [32, 256, 1024], P('br', None, 'own'), may hold values from -6 to 6
- branch_values: bfloat16 [32, 256, 1024], P('br', None, 'own'), may hold values from -6 to 6
- attn_out: bfloat16 [32, 256, 5120], P('br', None, 'own'), may hold values from -6 to 6
- out_grad: bfloat16 [32, 256, 5120], P('br', None, 'own'), may hold values from -6 to 6
- logsumexp: float32 [32, 40, 256], P('br', 'own'), may hold values from 7 to 8.5
- prefix_keys: bfloat16 [512, 4, 1024], P('br', 'own'), may hold values from -6 to 6
- prefix_values: bfloat16 [512, 4, 1024], P('br', 'own'), may hold values from -6 to 6
- prefix_of: int32 [32], P('br'), may hold values from 0 to 3
- counts: int32 [8], P('br'), may hold values from 1 to 4, as said below
Outputs:
- query_grad: bfloat16 [32, 256, 5120], P('br', None, 'own')
- key_grad: bfloat16 [32, 256, 1024], P('br', None, 'own')
- value_grad: bfloat16 [32, 256, 1024], P('br', None, 'own')
- prefix_key_grad: bfloat16 [512, 4, 1024], P('br', 'own')
- prefix_value_grad: bfloat16 [512, 4, 1024], P('br', 'own')
Inputs may be any that keep to these rules, and one draw needn't show every extreme that they name: The first counts[b] of the 4 slots of br index b hold branches, the other slots are empty; some br index is full in every draw.
All inputs are finite; a program needn't handle non-finite values.
Results may differ from a plain program's by a relative error of at most 0.0049.
Values may be sent and summed in bfloat16 or wider, within the bound.
A program may use at most 64 MiB of HBM per device.

v0:
```python
import jax
import jax.numpy as jnp
from jax import lax
from jax.sharding import PartitionSpec as P

QH = 40
KVH = 8
HD = 128


def per_device(
    queries,
    branch_keys,
    branch_values,
    attn_out,
    out_grad,
    logsumexp,
    prefix_keys,
    prefix_values,
    prefix_of,
    counts,
):
    slots, length, width = queries.shape
    kv_width = branch_keys.shape[2]
    kv_heads = kv_width // HD
    groups = QH // KVH
    scale = HD ** (-0.5)
    live_count = counts[0]
    alive = (jnp.arange(slots) < live_count).astype(jnp.float32)
    query5 = queries.reshape(slots, length, kv_heads, groups, HD)
    grad5 = out_grad.reshape(slots, length, kv_heads, groups, HD)
    product = out_grad.astype(jnp.float32) * attn_out.astype(jnp.float32)
    delta = jnp.sum(product.reshape(slots, length, kv_heads, groups, HD), axis=4).transpose(
        0, 2, 3, 1
    )
    lse5 = logsumexp.reshape(slots, kv_heads, groups, length)
    home_k, home_v = (
        lax.all_to_all(prefix_keys, "own", split_axis=2, concat_axis=1, tiled=True),
        lax.all_to_all(prefix_values, "own", split_axis=2, concat_axis=1, tiled=True),
    )
    total_rows = home_k.shape[0] * lax.axis_size("br")
    num_pre = home_k.shape[1]

    def slot_grads(c, key_block, val_block):
        rows = key_block.shape[0]
        pidx = prefix_of[c]
        pkey = lax.dynamic_index_in_dim(key_block, pidx, 1, keepdims=False).reshape(
            rows, kv_heads, HD
        )
        pval = lax.dynamic_index_in_dim(val_block, pidx, 1, keepdims=False).reshape(
            rows, kv_heads, HD
        )
        query_c = query5[c]
        grad_c = grad5[c]
        score = (
            jnp.einsum("lkgd,rkd->kglr", query_c, pkey, preferred_element_type=jnp.float32) * scale
        )
        prob = jnp.exp(score - lse5[c][..., None]) * alive[c]
        prob_b = prob.astype(jnp.bfloat16)
        dprob = jnp.einsum("lkgd,rkd->kglr", grad_c, pval, preferred_element_type=jnp.float32)
        dscore = (prob * (dprob - delta[c][..., None])).astype(jnp.bfloat16)
        dk = scale * jnp.einsum(
            "kglr,lkgd->rkd", dscore, query_c, preferred_element_type=jnp.float32
        )
        dv = jnp.einsum("kglr,lkgd->rkd", prob_b, grad_c, preferred_element_type=jnp.float32)
        rows_grad = jnp.concatenate([dk.reshape(rows, kv_width), dv.reshape(rows, kv_width)], 1)
        dq_term = None
        dq_term = scale * jnp.einsum(
            "kglr,rkd->lkgd", dscore, pkey, preferred_element_type=jnp.float32
        ).reshape(length, width)
        return (dq_term, rows_grad[:, None, :], pidx)

    def add_dq(dq_acc, c, term):
        old = lax.dynamic_index_in_dim(dq_acc, c, 0, keepdims=False)
        return lax.dynamic_update_index_in_dim(dq_acc, old + term, c, 0)

    def add_rows(dkv_acc, start, column, rows_grad):
        index = (start, column, 0)
        old = lax.dynamic_slice(dkv_acc, index, rows_grad.shape)
        return lax.dynamic_update_slice(dkv_acc, old + rows_grad, index)

    dq_zero = jnp.zeros((slots, length, width), jnp.float32)
    dkv_zero = jnp.zeros((total_rows, num_pre, 2 * kv_width), jnp.float32)
    start = jnp.int32(0)
    key_block = lax.all_gather(home_k, "br", axis=0, tiled=True)
    val_block = lax.all_gather(home_v, "br", axis=0, tiled=True)

    def one_slot(c, state):
        dq_acc, dkv_acc = state
        dq_term, rows_grad, pidx = slot_grads(c, key_block, val_block)
        return (add_dq(dq_acc, c, dq_term), add_rows(dkv_acc, start, pidx, rows_grad))

    dq_prefix, dkv_all = lax.fori_loop(0, slots, one_slot, (dq_zero, dkv_zero))
    summed = lax.psum_scatter(dkv_all, "br", scatter_dimension=0, tiled=True)
    causal = jnp.arange(length)[None, :] <= jnp.arange(length)[:, None]

    def self_slot(c, state):
        dq_acc, dk_acc, dv_acc = state
        query_c = query5[c]
        grad_c = grad5[c]
        bkey = branch_keys[c].reshape(length, kv_heads, HD)
        bval = branch_values[c].reshape(length, kv_heads, HD)
        score = (
            jnp.einsum("lkgd,rkd->kglr", query_c, bkey, preferred_element_type=jnp.float32) * scale
        )
        prob = jnp.where(causal, jnp.exp(score - lse5[c][..., None]), 0.0) * alive[c]
        prob_b = prob.astype(jnp.bfloat16)
        dprob = jnp.einsum("lkgd,rkd->kglr", grad_c, bval, preferred_element_type=jnp.float32)
        dscore = (prob * (dprob - delta[c][..., None])).astype(jnp.bfloat16)
        dq_term = scale * jnp.einsum(
            "kglr,rkd->lkgd", dscore, bkey, preferred_element_type=jnp.float32
        ).reshape(length, width)
        dk = scale * jnp.einsum(
            "kglr,lkgd->rkd", dscore, query_c, preferred_element_type=jnp.float32
        )
        dv = jnp.einsum("kglr,lkgd->rkd", prob_b, grad_c, preferred_element_type=jnp.float32)
        dq_acc = add_dq(dq_acc, c, dq_term)
        dk_acc = lax.dynamic_update_index_in_dim(
            dk_acc, dk.reshape(length, kv_width).astype(jnp.bfloat16), c, 0
        )
        dv_acc = lax.dynamic_update_index_in_dim(
            dv_acc, dv.reshape(length, kv_width).astype(jnp.bfloat16), c, 0
        )
        return (dq_acc, dk_acc, dv_acc)

    branch_zero = jnp.zeros((slots, length, kv_width), jnp.bfloat16)
    dq_total, key_grad, value_grad = lax.fori_loop(
        0, slots, self_slot, (dq_prefix, branch_zero, branch_zero)
    )
    query_grad = dq_total.astype(jnp.bfloat16)
    key_home = summed[:, :, :kv_width].astype(jnp.bfloat16)
    value_home = summed[:, :, kv_width:].astype(jnp.bfloat16)
    prefix_key_grad, prefix_value_grad = (
        lax.all_to_all(key_home, "own", split_axis=1, concat_axis=2, tiled=True),
        lax.all_to_all(value_home, "own", split_axis=1, concat_axis=2, tiled=True),
    )
    return (query_grad, key_grad, value_grad, prefix_key_grad, prefix_value_grad)


def solution(mesh):
    placed = (
        P("br", None, "own"),
        P("br", None, "own"),
        P("br", None, "own"),
        P("br", None, "own"),
        P("br", None, "own"),
        P("br", "own", None),
        P("br", "own", None),
        P("br", "own", None),
        P("br"),
        P("br"),
    )
    return jax.shard_map(
        per_device,
        mesh=mesh,
        in_specs=placed,
        out_specs=(
            P("br", None, "own"),
            P("br", None, "own"),
            P("br", None, "own"),
            P("br", "own", None),
            P("br", "own", None),
        ),
        check_vma=False,
    )
```

profile of v0, /device:TPU:0, one launch (start us, length us, event | category | flops | bytes accessed | tf_op | source)
XLA Modules:
  0.0 459.4 jit_solution(16943535065028473985)
XLA Ops:
  9.0 2.3 reduce
  11.5 10.0 %all_to_all.48 = bf16[4,2,8192]{2,1,0:T(2,128)(2,1)S(1)} all-to-all(bf16[4,2,8192]{2,1,0:T(2,128)(2,1)S(1)} %reshape.149), channel_id=1, replica_groups=mesh['own'=4,'br'=8] {'own'}, dimensions={0} | all-to-all | bytes 262144 | tf_op jit(solution)/shard_map/all_to_all | solution.py:38
  23.3 2.3 reduce.1
  25.9 7.4 %all_to_all.49 = bf16[4,2,8192]{2,1,0:T(2,128)(2,1)S(1)} all-to-all(bf16[4,2,8192]{2,1,0:T(2,128)(2,1)S(1)} %reshape.151), channel_id=1, replica_groups=mesh['own'=4,'br'=8] {'own'}, dimensions={0} | all-to-all | bytes 262144 | tf_op jit(solution)/shard_map/all_to_all | solution.py:39
  34.7 3.0 copy.123
  37.7 4.9 %copy.125 = bf16[4,256,1280]{1,2,0:T(8,128)(2,1)} copy(bf16[4,256,1280]{2,1,0:T(8,128)(2,1)} %param.17) | data formatting | bytes 5242880 | tf_op args[3]
  42.6 2.6 copy.130
  45.2 4.4 copy.120
  49.6 3.2 copy.127
  53.5 5.5 %convert_multiply_fusion = f32[4,256,1280]{1,2,0:T(8,128)} fusion(bf16[4,256,1280]{1,2,0:T(8,128)(2,1)} %copy.125, bf16[4,256,1280]{1,2,0:T(8,128)(2,1)} %copy-done.3), kind=kLoop, calls=%fused_computation.73 | loop fusion | flops 3932160 | bytes 10485760 | tf_op jit(solution)/shard_map/mul | solution.py:32
  59.0 3.0 reduce_sum.9
  63.3 2.4 copy.126
  65.8 3.0 all-gather.5.cloned.1.call-done
  68.8 2.4 copy.129
  71.2 2.7 broadcast_in_dim.48
  73.9 2.6 broadcast_in_dim.49.clone
  76.5 202.4 %while.33 = (s32[]{:T(128)}, f32[4,256,1280]{1,2,0:T(8,128)}, f32[512,4,512]{2,1,0:T(4,128)}, s32[4]{0:T(128)S(1)}, bf16[512,4,256]{0,2,1:T(8,128)(2,1)}, /*inde...) while((s32[]{:T(128)}, f32[4,256,1280]{1,2,0:T(8,128)}, ...), condition=%wide.region_2.3_spmd, body=%wide.region_1.2_spmd.sunk | while | flops 1692139520 | bytes 77423928 | solution.py:93
  86.3 2.8 fusion.109
  89.0 4.0 constant_dynamic-slice_fusion.9
  93.1 3.6 copy.188
  96.7 2.6 fusion.111
  99.3 3.6 copy.189
  102.9 21.0 %dynamic_update_slice.50 = f32[512,4,512]{2,1,0:T(4,128)} dynamic-update-slice(f32[512,4,512]{2,1,0:T(4,128)} %get-tuple-element.726, f32[512,1,512]{2,1,0:T(1,128)} %copy.189, s32[]{:T(128)} %constant.96.clone.1..sunk, s32[]{:T(128)S(6)} %select_n.65, s32[]{:T(128)} %constant.96.clone.1..sunk) | dynamic-update-slice | bytes 2097156 | tf_op jit(solution)/shard_map/while/body/eval_jaxpr/dynamic_update_slice | solution.py:80
  124.4 2.7 add_dynamic-update-slice_fusion.4
  136.9 2.8 fusion.109
  139.6 4.0 constant_dynamic-slice_fusion.9
  143.7 3.6 copy.188
  147.3 2.6 fusion.111
  149.9 3.6 copy.189
  153.5 21.0 %dynamic_update_slice.50 = f32[512,4,512]{2,1,0:T(4,128)} dynamic-update-slice(f32[512,4,512]{2,1,0:T(4,128)} %get-tuple-element.726, f32[512,1,512]{2,1,0:T(1,128)} %copy.189, s32[]{:T(128)} %constant.96.clone.1..sunk, s32[]{:T(128)S(6)} %select_n.65, s32[]{:T(128)} %constant.96.clone.1..sunk) | dynamic-update-slice | bytes 2097156 | tf_op jit(solution)/shard_map/while/body/eval_jaxpr/dynamic_update_slice | solution.py:80
  175.0 2.7 add_dynamic-update-slice_fusion.4
  183.2 2.2 fusion.108
  187.5 2.8 fusion.109
  190.2 4.0 constant_dynamic-slice_fusion.9
  194.3 3.6 copy.188
  197.9 2.6 fusion.111
  200.5 3.6 copy.189
  204.1 21.0 %dynamic_update_slice.50 = f32[512,4,512]{2,1,0:T(4,128)} dynamic-update-slice(f32[512,4,512]{2,1,0:T(4,128)} %get-tuple-element.726, f32[512,1,512]{2,1,0:T(1,128)} %copy.189, s32[]{:T(128)} %constant.96.clone.1..sunk, s32[]{:T(128)S(6)} %select_n.65, s32[]{:T(128)} %constant.96.clone.1..sunk) | dynamic-update-slice | bytes 2097156 | tf_op jit(solution)/shard_map/while/body/eval_jaxpr/dynamic_update_slice | solution.py:80
  225.6 2.7 add_dynamic-update-slice_fusion.4
  238.1 2.8 fusion.109
  240.8 4.0 constant_dynamic-slice_fusion.9
  244.9 3.6 copy.188
  248.5 2.6 fusion.111
  251.1 3.6 copy.189
  254.7 21.0 %dynamic_update_slice.50 = f32[512,4,512]{2,1,0:T(4,128)} dynamic-update-slice(f32[512,4,512]{2,1,0:T(4,128)} %get-tuple-element.726, f32[512,1,512]{2,1,0:T(1,128)} %copy.189, s32[]{:T(128)} %constant.96.clone.1..sunk, s32[]{:T(128)S(6)} %select_n.65, s32[]{:T(128)} %constant.96.clone.1..sunk) | dynamic-update-slice | bytes 2097156 | tf_op jit(solution)/shard_map/while/body/eval_jaxpr/dynamic_update_slice | solution.py:80
  276.2 2.7 add_dynamic-update-slice_fusion.4
  278.9 88.9 %all-reduce.2 = bf16[512,4,512]{2,1,0:T(4,128)(2,1)} all-reduce(f32[512,4,512]{2,1,0:T(4,128)} %get-tuple-element.395), channel_id=2, replica_groups=mesh['own'=4,'br'=8] {'br'}, use_global_device_ids=true, to_apply=%region_5.6.clone | all-reduce | flops 1048576 | bytes 6291456
  369.6 3.6 all-to-all-start.2
  373.9 4.3 all-to-all-done.2
  378.3 3.5 all-to-all-start.3
  381.8 64.1 %while.34 = (s32[]{:T(128)}, f32[4,256,1280]{1,2,0:T(8,128)}, bf16[4,256,256]{2,1,0:T(8,128)(2,1)}, bf16[4,256,256]{2,1,0:T(8,128)(2,1)}, bf16[4,256,256]{2,1,0:...) while((s32[]{:T(128)}, f32[4,256,1280]{1,2,0:T(8,128)}, ...), condition=%wide.region_4.5_spmd.clone, body=%wide.region_3.4_spmd.clone.sunk | while | flops 847642624 | bytes 22685328 | solution.py:127
  385.7 3.6 fusion.123
  389.7 2.6 add_dynamic-update-slice_fusion.5
  393.6 3.5 fusion.125
  401.8 3.6 fusion.123
  405.7 2.6 add_dynamic-update-slice_fusion.5
  409.6 3.5 fusion.125
  417.8 3.6 fusion.123
  421.7 2.6 add_dynamic-update-slice_fusion.5
  425.7 3.5 fusion.125
  433.8 3.6 fusion.123
  437.8 2.5 add_dynamic-update-slice_fusion.5
  441.7 3.5 fusion.125
  445.9 4.9 %copy.136 = bf16[4,256,1280]{2,1,0:T(8,128)(2,1)} copy(f32[4,256,1280]{1,2,0:T(8,128)} %get-tuple-element.392) | data formatting | bytes 7864320 | tf_op jit(solution)/shard_map/while | solution.py:127
  (147 shorter events, 66.4 us)
Async XLA Ops:
  7.2 15.8 %copy-start.4 = (bf16[64,1,1024]{2,0,1:T(8,128)(2,1)S(1)}, bf16[64,1,1024]{2,0,1:T(8,128)(2,1)}, u32[]{:S(2)}) copy-start(bf16[64,1,1024]{2,0,1:T(8,128)(2,1)} %param.21) | copy-start | bytes 393220
  7.2 56.1 %all-gather.3.cloned.1.call-start = ((), (), s32[]{:S(2)}) async-start(), calls=%async_computation.4 | async-start | bytes 1179648 | tf_op jit(solution)/shard_map/all_gather | solution.py:85
  22.9 45.9 %all-gather.5.cloned.1.call-start = ((), (), s32[]{:S(2)}) async-start(), calls=%async_computation.5 | async-start | bytes 1179648 | tf_op jit(solution)/shard_map/all_gather | solution.py:86
  37.7 4.9 %copy-start.3 = (bf16[4,256,1280]{1,2,0:T(8,128)(2,1)}, bf16[4,256,1280]{1,2,0:T(8,128)(2,1)S(1)}, u32[]{:S(2)}) copy-start(bf16[4,256,1280]{1,2,0:T(8,128)(2,1)S(1)} %copy.123) | copy-start | bytes 7864324
  49.6 3.2 copy-start.5
  59.0 3.0 copy-start.7
  73.9 2.6 copy-start.6
  76.5 4.6 %copy-start = (bf16[4,256,2,5,128]{4,1,3,2,0:T(8,128)(2,1)}, bf16[4,256,2,5,128]{4,1,3,2,0:T(8,128)(2,1)S(1)}, u32[]{:S(2)}) copy-start(bf16[4,256,2,5,128]{4,1,3,2,0:T(8,128)(2,1)S(1)} %get-tuple-element.743) | copy-start | bytes 7864324 | tf_op jit(solution)/shard_map/while
  80.2 1.7 copy-start.2
  124.4 2.7 copy-start.1
  127.1 4.6 %copy-start = (bf16[4,256,2,5,128]{4,1,3,2,0:T(8,128)(2,1)}, bf16[4,256,2,5,128]{4,1,3,2,0:T(8,128)(2,1)S(1)}, u32[]{:S(2)}) copy-start(bf16[4,256,2,5,128]{4,1,3,2,0:T(8,128)(2,1)S(1)} %get-tuple-element.743) | copy-start | bytes 7864324 | tf_op jit(solution)/shard_map/while
  130.8 1.7 copy-start.2
  175.0 2.7 copy-start.1
  177.7 4.6 %copy-start = (bf16[4,256,2,5,128]{4,1,3,2,0:T(8,128)(2,1)}, bf16[4,256,2,5,128]{4,1,3,2,0:T(8,128)(2,1)S(1)}, u32[]{:S(2)}) copy-start(bf16[4,256,2,5,128]{4,1,3,2,0:T(8,128)(2,1)S(1)} %get-tuple-element.743) | copy-start | bytes 7864324 | tf_op jit(solution)/shard_map/while
  181.4 1.7 copy-start.2
  225.6 2.7 copy-start.1
  228.3 4.6 %copy-start = (bf16[4,256,2,5,128]{4,1,3,2,0:T(8,128)(2,1)}, bf16[4,256,2,5,128]{4,1,3,2,0:T(8,128)(2,1)S(1)}, u32[]{:S(2)}) copy-start(bf16[4,256,2,5,128]{4,1,3,2,0:T(8,128)(2,1)S(1)} %get-tuple-element.743) | copy-start | bytes 7864324 | tf_op jit(solution)/shard_map/while
  232.0 1.7 copy-start.2
  276.2 2.7 copy-start.1
  369.6 8.7 %all-to-all-start.2 = ((bf16[64,4,256]{2,0,1:T(8,128)(2,1)}), bf16[64,4,256]{2,0,1:T(8,128)(2,1)S(1)}, u32[]{:S(2)}, u32[]{:S(2)}) async-start(bf16[64,4,256]{2,0,1:T(8,128)(2,1)} %copy.138), calls=%async_computation.2 | async-start | bytes 262144 | tf_op jit(solution)/shard_map/all_to_all | solution.py:134
  378.3 73.4 %all-to-all-start.3 = ((bf16[64,4,256]{2,0,1:T(8,128)(2,1)}), bf16[64,4,256]{2,0,1:T(8,128)(2,1)S(1)}, u32[]{:S(2)}, u32[]{:S(2)}) async-start(bf16[64,4,256]{2,0,1:T(8,128)(2,1)} %copy.140), calls=%async_computation.3 | async-start | bytes 262144 | tf_op jit(solution)/shard_map/all_to_all | solution.py:135
Sparse Core Ops, SparseCore 0:
  23.0 21.8 all-gather.2
  47.0 21.7 all-gather.4
where the time goes:
time: 464 us; the launch traced here: 459 us
  local copies, waits for them, and re-layouts  196 us (42%)
  blocking collectives  106 us (23%)
  matrix products  74.1 us (16%)
  other arithmetic  44.5 us (10%)
  between operations  15.5 us (3%)
  loops' own time  8.45 us (2%)
  waiting for transfers between devices  7.44 us (2%)
  starting transfers between devices  7.25 us (2%)
    dynamic_update_slice x8, local copies, waits for them, and re-layouts, add_rows(): return lax.dynamic_update_slice(dkv_acc, old + rows_grad, index)  98.4 us
    unnamed x1, blocking collectives  88.9 us
    dynamic_slice x8, local copies, waits for them, and re-layouts, add_rows(): old = lax.dynamic_slice(dkv_acc, index, rows_grad.shape)  30.6 us
    dynamic_update_slice x8, other arithmetic, add_dq(): return lax.dynamic_update_index_in_dim(dq_acc, old + term, c, 0)  21 us
    unnamed x21, local copies, waits for them, and re-layouts  16.1 us
    dot_general x4, matrix products, self_slot(): jnp.einsum('lkgd,rkd->kglr', grad_c, bval, preferred_element_type=jnp.flo...  14.4 us
    dot_general x4, matrix products, self_slot(): jnp.einsum('kglr,lkgd->rkd', prob_b, grad_c, preferred_element_type=jnp.f...  13.9 us
    dot_general x4, matrix products, slot_grads(): jnp.einsum('kglr,lkgd->rkd', prob_b, grad_c, preferred_element_type=jnp.f...  11 us
  transfers between devices with their start and end apart: 4, of which 2 were waited for; matrix products, arithmetic and copies ran while one was open for 22% of the time, Pallas kernels for 0%

commit v1 on v0

v1 whole, which is shorter than its diff:
```python
import functools

import jax
import jax.numpy as jnp
from jax import lax
from jax.experimental import pallas as pl
from jax.experimental.pallas import tpu as pltpu
from jax.sharding import PartitionSpec as P

QH = 40
KVH = 8
HD = 128
GROUPS = QH // KVH
LOG2E = 1.4426950408889634
SCALE = HD ** (-0.5)
DEAD = 1e30

MESH = pl.DeviceIdType.MESH


def flip(index, bits):
    out, bit = index, 1
    while bit <= bits:
        if bits & bit:
            out = out + bit * (1 - 2 * ((index // bit) % 2))
        bit *= 2
    return out


def dot_nt(a, b):
    return lax.dot_general(a, b, (((1,), (1,)), ((), ())), preferred_element_type=jnp.float32)


def dot(a, b):
    return jnp.dot(a, b, preferred_element_type=jnp.float32)


def kernel(
    n_own,
    planes,
    pref_ref,
    w_ref,
    src,
    q_ref,
    bk_ref,
    bv_ref,
    ao_ref,
    og_ref,
    lse_ref,
    qg_ref,
    kg_ref,
    vg_ref,
    pk_ref,
    pv_ref,
    g0,
    g1,
    dqt,
    delta,
    acc,
    mine0,
    mine1,
    out0,
    out1,
    in0,
    in1,
    pre0,
    pre1,
    land,
    g_send,
    g_recv,
    f_send,
    f_recv,
    local_sem,
    s_send,
    s_recv,
    r_send,
    r_recv,
):
    slots, length, _ = q_ref.shape
    kv_heads = bk_ref.shape[2] // HD
    cw = kv_heads * HD
    ppo, rows = src.shape[1], src.shape[2]
    num_pre = n_own * ppo
    half = planes // 2
    chunk_rows = half * 2 * rows
    own = lax.axis_index("own")
    br = lax.axis_index("br")
    plane, core = br // 2, br % 2
    gathered, mine, outgoing, incoming, presum = (
        (g0, g1),
        (mine0, mine1),
        (out0, out1),
        (in0, in1),
        (pre0, pre1),
    )

    def device(d, j):
        return {"own": flip(own, j), "br": flip(plane, d) * 2 + core}

    sibling = {"own": own, "br": plane * 2 + 1 - core}
    peers = [(d, j) for d in range(planes) for j in range(n_own) if (d, j) != (0, 0)]

    barrier = pltpu.get_barrier_semaphore()
    for d, j in peers:
        pl.semaphore_signal(barrier, inc=1, device_id=device(d, j), device_id_type=MESH)
    pl.semaphore_signal(barrier, inc=1, device_id=sibling, device_id_type=MESH)
    pl.semaphore_wait(barrier, len(peers) + 1)

    def place(d, o, side):
        return gathered[d // half].at[pl.ds(o * ppo, ppo), 2 * (d % half) + side]

    def gather_copy(d, j):
        return pltpu.make_async_remote_copy(
            src_ref=src.at[flip(own, j)],
            dst_ref=place(d, own, 0),
            send_sem=g_send.at[d, j],
            recv_sem=g_recv.at[d, j],
            device_id=device(d, j),
            device_id_type=MESH,
        )

    def forward_copy(d, j):
        o = flip(own, j)
        return pltpu.make_async_remote_copy(
            src_ref=src.at[own] if (d, j) == (0, 0) else place(d, o, 0),
            dst_ref=place(d, o, 1),
            send_sem=f_send.at[d, j],
            recv_sem=f_recv.at[d, j],
            device_id=sibling,
            device_id_type=MESH,
        )

    local = pltpu.make_async_copy(src.at[own], place(0, own, 0), local_sem)
    local.start()
    for d, j in reversed(peers):
        gather_copy(d, j).start()
    forward_copy(0, 0).start()

    def head_cols(k, h):
        return pl.ds(pl.multiple_of(k * (GROUPS * HD) + h * HD, HD), HD)

    def kv_cols(k, base):
        return pl.ds(pl.multiple_of(base + k * HD, HD), HD)

    def grads(c, k, key, val, causal, use_dq):
        key_t = key.T
        dk = dv = None
        for h in range(GROUPS):
            query = q_ref[c, :, head_cols(k, h)]
            grad = og_ref[c, :, head_cols(k, h)]
            lse = lse_ref[c, k, pl.ds(h, 1), :]
            if causal is not None:
                product = grad.astype(jnp.float32) * ao_ref[c, :, head_cols(k, h)].astype(
                    jnp.float32
                )
                dlt = jnp.sum(product.T, axis=0, keepdims=True)
                delta[c, k, pl.ds(h, 1), :] = dlt
            else:
                dlt = delta[c, k, pl.ds(h, 1), :]
            prob = jnp.exp2(dot_nt(key, query) * (SCALE * LOG2E) - lse)
            if causal is not None:
                prob = jnp.where(causal, prob, 0.0)
            dscore = (prob * (dot_nt(val, grad) - dlt)).astype(jnp.bfloat16)
            dk_h = dot(dscore, query)
            dv_h = dot(prob.astype(jnp.bfloat16), grad)
            dk = dk_h if dk is None else dk + dk_h
            dv = dv_h if dv is None else dv + dv_h
            use_dq(h, dot(key_t, dscore))
        return dk * SCALE, dv

    causal = lax.broadcasted_iota(jnp.int32, (length, length), 0) <= lax.broadcasted_iota(
        jnp.int32, (length, length), 1
    )

    def branch_step(step, carry):
        c, k = step // kv_heads, step % kv_heads

        def use_dq(h, term):
            dqt[c, k, h] = term

        dk, dv = grads(
            c, k, bk_ref[c, :, kv_cols(k, 0)], bv_ref[c, :, kv_cols(k, 0)], causal, use_dq
        )
        kg_ref[c, :, kv_cols(k, 0)] = dk.astype(jnp.bfloat16)
        vg_ref[c, :, kv_cols(k, 0)] = dv.astype(jnp.bfloat16)
        return carry

    lax.fori_loop(0, slots * kv_heads, branch_step, 0)

    def arrive(chunk):
        here = [(d, j) for d, j in peers if d // half == chunk]
        for d, j in here:
            gather_copy(d, j).wait_recv()
            forward_copy(d, j).start()
        if chunk == 0:
            local.wait()
            here = here + [(0, 0)]
        for d, j in here:
            forward_copy(d, j).wait_recv()

    def prefix_chunk(chunk):
        buf = gathered[chunk]

        def prefix_step(step, carry):
            c, k = step // kv_heads, step % kv_heads
            p = pref_ref[c]
            key = buf[p, :, :, kv_cols(k, 0)].reshape(chunk_rows, HD)
            val = buf[p, :, :, kv_cols(k, cw)].reshape(chunk_rows, HD)

            def use_dq(h, term):
                total = dqt[c, k, h] + term
                if chunk == 0:
                    dqt[c, k, h] = total
                else:
                    qg_ref[c, :, head_cols(k, h)] = (total * SCALE).T.astype(jnp.bfloat16)

            dk, dv = grads(c, k, key, val, None, use_dq)
            acc[c, :, kv_cols(k, 0)] = dk
            acc[c, :, kv_cols(k, cw)] = dv
            return carry

        lax.fori_loop(0, slots * kv_heads, prefix_step, 0)

        def combine(dd, carry):
            for side, target in ((0, mine[chunk]), (1, outgoing[chunk])):
                start = pl.multiple_of((dd * 2 + side) * rows, rows)
                parts = [acc[c, pl.ds(start, rows), :] for c in range(slots)]
                for p in range(num_pre):
                    total = parts[0] * w_ref[0, p]
                    for c in range(1, slots):
                        total = total + parts[c] * w_ref[c, p]
                    target[dd, p] = total.astype(target.dtype)
            return carry

        lax.fori_loop(0, half, combine, 0)

    def sibling_copy(chunk):
        return pltpu.make_async_remote_copy(
            src_ref=outgoing[chunk],
            dst_ref=incoming[chunk],
            send_sem=s_send.at[chunk],
            recv_sem=s_recv.at[chunk],
            device_id=sibling,
            device_id_type=MESH,
        )

    def reduce_copy(d, j):
        return pltpu.make_async_remote_copy(
            src_ref=presum[d // half].at[d % half, pl.ds(flip(own, j) * ppo, ppo)],
            dst_ref=land.at[d, own],
            send_sem=r_send.at[d, j],
            recv_sem=r_recv.at[d, j],
            device_id=device(d, j),
            device_id_type=MESH,
        )

    def send_sums(chunk):
        sibling_copy(chunk).wait_recv()

        def add(dd, carry):
            for p in range(num_pre):
                presum[chunk][dd, p] = (
                    mine[chunk][dd, p] + incoming[chunk][dd, p].astype(jnp.float32)
                ).astype(jnp.bfloat16)
            return carry

        lax.fori_loop(0, half, add, 0)
        for d, j in reversed(peers):
            if d // half == chunk:
                reduce_copy(d, j).start()
        if chunk == 0:
            land[0, own] = presum[0][0, pl.ds(own * ppo, ppo)]

    arrive(0)
    prefix_chunk(0)
    sibling_copy(0).start()
    arrive(1)
    send_sums(0)
    prefix_chunk(1)
    sibling_copy(1).start()
    send_sums(1)

    for d, j in peers:
        reduce_copy(d, j).wait_recv()

    for o in range(n_own):
        for i in range(ppo):
            total = land[0, o, i].astype(jnp.float32)
            for d in range(1, planes):
                total = total + land[d, o, i].astype(jnp.float32)
            pk_ref[i, :, o * cw : (o + 1) * cw] = total[:, :cw].astype(jnp.bfloat16)
            pv_ref[i, :, o * cw : (o + 1) * cw] = total[:, cw:].astype(jnp.bfloat16)

    forward_copy(0, 0).wait_send()
    for d, j in peers:
        gather_copy(d, j).wait_send()
        forward_copy(d, j).wait_send()
        reduce_copy(d, j).wait_send()
    for chunk in (0, 1):
        sibling_copy(chunk).wait_send()


def per_device(
    queries,
    branch_keys,
    branch_values,
    attn_out,
    out_grad,
    logsumexp,
    prefix_keys,
    prefix_values,
    prefix_of,
    counts,
    *,
    n_own,
    n_br,
):
    slots, length, width = queries.shape
    cw = branch_keys.shape[2]
    kv_heads = cw // HD
    rows, ppo, _ = prefix_keys.shape
    num_pre = n_own * ppo
    planes = n_br // 2
    half = planes // 2
    alive = jnp.arange(slots) < counts[0]
    lse = jnp.where(alive[:, None, None], logsumexp * LOG2E, DEAD).reshape(
        slots, kv_heads, GROUPS, length
    )
    weights = (prefix_of[:, None] == jnp.arange(num_pre)[None, :]).astype(jnp.float32)
    kv = jnp.concatenate(
        [
            prefix_keys.reshape(rows, ppo, n_own, cw),
            prefix_values.reshape(rows, ppo, n_own, cw),
        ],
        axis=3,
    ).transpose(2, 1, 0, 3)

    bf16, f32 = jnp.bfloat16, jnp.float32
    vmem = pl.BlockSpec(memory_space=pltpu.VMEM)
    smem = pl.BlockSpec(memory_space=pltpu.SMEM)
    dma = pltpu.SemaphoreType.DMA
    part = (half, num_pre, rows, 2 * cw)
    query_grad, key_grad, value_grad, pk, pv = pl.pallas_call(
        functools.partial(kernel, n_own, planes),
        out_shape=(
            jax.ShapeDtypeStruct(queries.shape, bf16),
            jax.ShapeDtypeStruct(branch_keys.shape, bf16),
            jax.ShapeDtypeStruct(branch_keys.shape, bf16),
            jax.ShapeDtypeStruct((ppo, rows, n_own * cw), bf16),
            jax.ShapeDtypeStruct((ppo, rows, n_own * cw), bf16),
        ),
        in_specs=[smem, smem] + [vmem] * 7,
        out_specs=(vmem,) * 5,
        scratch_shapes=[
            pltpu.VMEM((num_pre, planes, rows, 2 * cw), bf16),
            pltpu.VMEM((num_pre, planes, rows, 2 * cw), bf16),
            pltpu.VMEM((slots, kv_heads, GROUPS, HD, length), f32),
            pltpu.VMEM((slots, kv_heads, GROUPS, length), f32),
            pltpu.VMEM((slots, planes * rows, 2 * cw), f32),
            pltpu.VMEM(part, f32),
            pltpu.VMEM(part, f32),
            pltpu.VMEM(part, bf16),
            pltpu.VMEM(part, bf16),
            pltpu.VMEM(part, bf16),
            pltpu.VMEM(part, bf16),
            pltpu.VMEM(part, bf16),
            pltpu.VMEM(part, bf16),
            pltpu.VMEM((planes, n_own, ppo, rows, 2 * cw), bf16),
            dma((planes, n_own)),
            dma((planes, n_own)),
            dma((planes, n_own)),
            dma((planes, n_own)),
            dma(()),
            dma((2,)),
            dma((2,)),
            dma((planes, n_own)),
            dma((planes, n_own)),
        ],
        compiler_params=pltpu.CompilerParams(
            collective_id=0, has_side_effects=True, vmem_limit_bytes=56 * 1024 * 1024
        ),
    )(prefix_of, weights, kv, queries, branch_keys, branch_values, attn_out, out_grad, lse)
    return (
        query_grad,
        key_grad,
        value_grad,
        pk.transpose(1, 0, 2),
        pv.transpose(1, 0, 2),
    )


def solution(mesh):
    placed = (
        P("br", None, "own"),
        P("br", None, "own"),
        P("br", None, "own"),
        P("br", None, "own"),
        P("br", None, "own"),
        P("br", "own", None),
        P("br", "own", None),
        P("br", "own", None),
        P("br"),
        P("br"),
    )
    return jax.shard_map(
        functools.partial(per_device, n_own=mesh.shape["own"], n_br=mesh.shape["br"]),
        mesh=mesh,
        in_specs=placed,
        out_specs=(
            P("br", None, "own"),
            P("br", None, "own"),
            P("br", None, "own"),
            P("br", "own", None),
            P("br", "own", None),
        ),
        check_vma=False,
    )
```

time: 464 us -> 92.3 us (0.20)
  local copies, waits for them, and re-layouts: 196 us -> 8.04 us
  blocking collectives: 106 us -> 0 us
  Pallas kernels: 0 us -> 79.8 us
  matrix products: 74.1 us -> 0 us
  other arithmetic: 44.5 us -> 2.89 us
  between operations: 15.5 us -> 1.33 us
  loops' own time: 8.45 us -> 0 us
  waiting for transfers between devices: 7.44 us -> 0 us
  starting transfers between devices: 7.25 us -> 0 us
    dynamic_update_slice x24 -> x0, local copies, waits for them, and re-layouts: 105 us -> none  [the longest x8 98.4 us: add_rows(): return lax.dynamic_update_slice(dkv_acc, old + rows_grad, index)]
    unnamed x1 -> x0, blocking collectives: 88.9 us -> none
    pallas_call x0 -> x1, Pallas kernels: none -> 79.8 us  [per_device(): pl.pallas_call(functools.partial(kernel, n_own, planes), out_shape=(jax.S...]
    dot_general x40 -> x0, matrix products: 74.1 us -> none  [the longest x4 14.4 us: self_slot(): jnp.einsum('lkgd,rkd->kglr', grad_c, bval, preferred_element_type=jnp.flo...]
    dynamic_slice x36 -> x0, local copies, waits for them, and re-layouts: 47 us -> none  [the longest x8 30.6 us: add_rows(): old = lax.dynamic_slice(dkv_acc, index, rows_grad.shape)]
    dynamic_update_slice x8 -> x0, other arithmetic: 21 us -> none  [add_dq(): return lax.dynamic_update_index_in_dim(dq_acc, old + term, c, 0)]
    all_to_all x2 -> x0, blocking collectives: 17.4 us -> none  [the longest x1 9.99 us: per_device(): lax.all_to_all(prefix_keys, 'own', split_axis=2, concat_axis=1, tiled=True)]
    while x30 -> x0, local copies, waits for them, and re-layouts: 16.5 us -> none  [the longest x5 10.7 us: per_device(): dq_prefix, dkv_all = lax.fori_loop(0, slots, one_slot, (dq_zero, dkv_zero))]
  transfers between devices with their start and end apart: 4 -> 0, of which waited for: 2 -> 0; matrix products, arithmetic and copies ran while one was open for 22% -> 0% of each run, Pallas kernels for 0% -> 0%
where the time goes in v1:
time: 92.3 us; the launch traced here: 92 us
  Pallas kernels  79.8 us (86%)
  local copies, waits for them, and re-layouts  8.04 us (9%)
  other arithmetic  2.89 us (3%)
  between operations  1.33 us (1%)
    pallas_call x1, Pallas kernels, per_device(): pl.pallas_call(functools.partial(kernel, n_own, planes), out_shape=(jax.S...  79.8 us
    unnamed x13, local copies, waits for them, and re-layouts  6.41 us

profile of v1, /device:TPU:0, one launch (start us, length us, event | category | flops | bytes accessed | tf_op | source)
XLA Modules:
  0.0 92.0 jit_solution(9070041500330831404)
XLA Ops:
  1.3 1.3 %fusion.w_ref = f32[4,4]{1,0:T(4,128)} fusion(s32[4]{0:T(128)} %pref_ref.1), kind=kLoop, calls=%fused_computation.5 | loop fusion | flops 32 | bytes 80 | tf_op jit(solution)/shard_map/convert_element_type | solution.py:329
  2.6 0.9 multiply_select_fusion
  3.4 0.6 copy.18.lse_ref
  4.1 1.0 %copy_bitcast_fusion = (bf16[64,1,4,256]{3,0,1,2:T(8,128)(2,1)S(1)}, bf16[64,1,4,256]{3,0,1,2:T(8,128)(2,1)S(1)}) fusion(bf16[1,8,4,8,256]{4,3,2,1,0:T(8,128)(2,1)} %bitcast.16, bf16[1,8,4,8,256]{4,3,2,1,0:T(8,128)(2,1)} %bitcast.17), kind=kLoop, calls=%fused_computation.1 | loop fusion | bytes 524288 | tf_op jit(solution)/shard_map/reshape | solution.py:333
  5.1 0.7 maximum_bitcast_fusion.src
  5.8 79.8 %shard_map.137 = (bf16[4,256,1280]{2,1,0:T(8,128)(2,1)}, bf16[4,256,256]{2,1,0:T(8,128)(2,1)}, bf16[4,256,256]{2,1,0:T(8,128)(2,1)}, bf16[1,64,1024]{2,1,0:T(8,128)(2,1)}, bf16[1,64,1024]{2,1,0:T(8,128)(2,1)}) custom-call(s32[4]{0:T(128)} %pref_ref.1, f32[4,4]{1,0:T(4,128)} %fusion.w_ref, bf16[4,1,64,512]{3,2,1,0:T(8,128)(2,1)} %maximum_bitcast_fusion.src, ...), custom_call_target="tpu_custom_call" | custom-call | tf_op jit(solution)/shard_map/pallas_call | solution.py:343
  85.6 0.0 copy-start.1
  85.6 0.0 copy-start
  85.6 0.0 copy-start.3
  85.6 0.0 copy-start.2
  85.6 3.5 %copy.29 = bf16[4,256,1280]{2,1,0:T(8,128)(2,1)} copy(bf16[4,256,1280]{2,1,0:T(8,128)(2,1)} %get-tuple-element.22) | data formatting | bytes 5242880
  89.1 0.0 copy-done.1
  89.1 0.8 copy.30
  89.9 0.0 copy-done
  89.9 0.8 copy.31
  90.7 0.0 copy-done.3
  90.7 0.7 copy.32
  91.4 0.0 copy-done.2
  91.4 0.7 copy.33
  (1 shorter events, 0.0 us)
Async XLA Ops:
  85.6 3.5 %copy-start.1 = (bf16[4,256,256]{2,1,0:T(8,128)(2,1)S(1)}, bf16[4,256,256]{2,1,0:T(8,128)(2,1)}, u32[]{:S(2)}) copy-start(bf16[4,256,256]{2,1,0:T(8,128)(2,1)} %get-tuple-element.23) | copy-start | bytes 1572868
  85.6 4.3 %copy-start = (bf16[4,256,256]{2,1,0:T(8,128)(2,1)S(1)}, bf16[4,256,256]{2,1,0:T(8,128)(2,1)}, u32[]{:S(2)}) copy-start(bf16[4,256,256]{2,1,0:T(8,128)(2,1)} %get-tuple-element.24) | copy-start | bytes 1572868
  85.6 5.1 %copy-start.3 = (bf16[1,64,1024]{2,1,0:T(8,128)(2,1)S(1)}, bf16[1,64,1024]{2,1,0:T(8,128)(2,1)}, u32[]{:S(2)}) copy-start(bf16[1,64,1024]{2,1,0:T(8,128)(2,1)} %get-tuple-element.13) | copy-start | bytes 393220
  85.6 5.8 %copy-start.2 = (bf16[1,64,1024]{2,1,0:T(8,128)(2,1)S(1)}, bf16[1,64,1024]{2,1,0:T(8,128)(2,1)}, u32[]{:S(2)}) copy-start(bf16[1,64,1024]{2,1,0:T(8,128)(2,1)} %get-tuple-element.14) | copy-start | bytes 393220

commit v2 on v1

v2 whole, which is shorter than its diff:
```python
import functools

import jax
import jax.numpy as jnp
from jax import lax
from jax.experimental import pallas as pl
from jax.experimental.pallas import tpu as pltpu
from jax.sharding import PartitionSpec as P

QH = 40
KVH = 8
HD = 128
GROUPS = QH // KVH
LOG2E = 1.4426950408889634
SCALE = HD ** (-0.5)
DEAD = 1e30

MESH = pl.DeviceIdType.MESH


def flip(index, bits):
    out, bit = index, 1
    while bit <= bits:
        if bits & bit:
            out = out + bit * (1 - 2 * ((index // bit) % 2))
        bit *= 2
    return out


def dot_nt(a, b):
    return lax.dot_general(a, b, (((1,), (1,)), ((), ())), preferred_element_type=jnp.float32)


def dot(a, b):
    return jnp.dot(a, b, preferred_element_type=jnp.float32)


def kernel(
    n_own,
    planes,
    pref_ref,
    count_ref,
    pkey_ref,
    pval_ref,
    lse_ref,
    q_hbm,
    bk_hbm,
    bv_hbm,
    ao_hbm,
    og_hbm,
    qg_ref,
    kg_ref,
    vg_ref,
    pk_ref,
    pv_ref,
    q_ref,
    bk_ref,
    bv_ref,
    ao_ref,
    og_ref,
    src,
    g0,
    g1,
    dqt,
    delta,
    lse2,
    acc,
    *rest,
):
    slots, length, _ = q_ref.shape
    kv_heads = bk_ref.shape[2] // HD
    cw = kv_heads * HD
    ppo, rows = src.shape[1], src.shape[2]
    num_pre = n_own * ppo
    half = planes // 2
    chunk_rows = half * 2 * rows
    own = lax.axis_index("own")
    br = lax.axis_index("br")
    plane, core = br // 2, br % 2
    gathered = (g0, g1)
    units = [(0, 0, kv_heads)] + [(1, k, k + 1) for k in range(kv_heads)]
    count = len(units)
    mine, outgoing, incoming, presum, land = (
        rest[i * count : (i + 1) * count] for i in range(5)
    )
    (
        load_sem,
        g_send,
        g_recv,
        f_send,
        f_recv,
        local_sem,
        s_send,
        s_recv,
        r_send,
        r_recv,
    ) = rest[5 * count :]

    def device(d, j):
        return {"own": flip(own, j), "br": flip(plane, d) * 2 + core}

    sibling = {"own": own, "br": plane * 2 + 1 - core}
    peers = [(d, j) for d in range(planes) for j in range(n_own) if (d, j) != (0, 0)]

    barrier = pltpu.get_barrier_semaphore()
    for d, j in peers:
        pl.semaphore_signal(barrier, inc=1, device_id=device(d, j), device_id_type=MESH)
    pl.semaphore_signal(barrier, inc=1, device_id=sibling, device_id_type=MESH)

    loads = [
        pltpu.make_async_copy(hbm, ref, load_sem.at[i])
        for i, (hbm, ref) in enumerate(
            (
                (og_hbm, og_ref),
                (ao_hbm, ao_ref),
                (q_hbm, q_ref),
                (bk_hbm, bk_ref),
                (bv_hbm, bv_ref),
            )
        )
    ]
    for load in loads:
        load.start()

    for o in range(n_own):
        for i in range(ppo):
            for k in range(kv_heads):
                start = o * cw + k * HD
                src[o, i, :, 2 * k * HD : (2 * k + 1) * HD] = pkey_ref[i, :, start : start + HD]
                src[o, i, :, (2 * k + 1) * HD : (2 * k + 2) * HD] = pval_ref[
                    i, :, start : start + HD
                ]

    pl.semaphore_wait(barrier, len(peers) + 1)

    def place(d, o, side):
        return gathered[d // half].at[pl.ds(o * ppo, ppo), 2 * (d % half) + side]

    def gather_copy(d, j):
        return pltpu.make_async_remote_copy(
            src_ref=src.at[flip(own, j)],
            dst_ref=place(d, own, 0),
            send_sem=g_send.at[d, j],
            recv_sem=g_recv.at[d, j],
            device_id=device(d, j),
            device_id_type=MESH,
        )

    def forward_copy(d, j):
        o = flip(own, j)
        return pltpu.make_async_remote_copy(
            src_ref=src.at[own] if (d, j) == (0, 0) else place(d, o, 0),
            dst_ref=place(d, o, 1),
            send_sem=f_send.at[d, j],
            recv_sem=f_recv.at[d, j],
            device_id=sibling,
            device_id_type=MESH,
        )

    for d, j in peers:
        gather_copy(d, j).start()
    forward_copy(0, 0).start()
    local = pltpu.make_async_copy(src.at[own], place(0, own, 0), local_sem)
    local.start()

    def head_cols(k, h):
        return pl.ds(pl.multiple_of(k * (GROUPS * HD) + h * HD, HD), HD)

    def kv_cols(k, base):
        return pl.ds(pl.multiple_of(base + k * HD, HD), HD)

    def pair_cols(k, second):
        return pl.ds(pl.multiple_of(k * (2 * HD) + second * HD, HD), HD)

    loads[0].wait()
    loads[1].wait()

    def prepare(step, carry):
        c, k = step // kv_heads, step % kv_heads
        dead = jnp.where(c < count_ref[0], 0.0, DEAD)
        for h in range(GROUPS):
            grad = og_ref[c, :, head_cols(k, h)].astype(jnp.float32)
            product = grad * ao_ref[c, :, head_cols(k, h)].astype(jnp.float32)
            delta[c, k, pl.ds(h, 1), :] = jnp.sum(product.T, axis=0, keepdims=True)
            lse2[c, k, pl.ds(h, 1), :] = lse_ref[c, pl.ds(k * GROUPS + h, 1), :] * LOG2E + dead
            dqt[c, k, h] = jnp.zeros((HD, length), jnp.float32)
        return carry

    lax.fori_loop(0, slots * kv_heads, prepare, 0)
    for load in loads[2:]:
        load.wait()

    def grads(c, k, key, val, causal):
        key_t = key.T
        dk = dv = None
        for h in range(GROUPS):
            query = q_ref[c, :, head_cols(k, h)]
            grad = og_ref[c, :, head_cols(k, h)]
            prob = jnp.exp2(
                dot_nt(key, query) * (SCALE * LOG2E) - lse2[c, k, pl.ds(h, 1), :]
            )
            if causal is not None:
                prob = jnp.where(causal, prob, 0.0)
            dscore = (prob * (dot_nt(val, grad) - delta[c, k, pl.ds(h, 1), :])).astype(
                jnp.bfloat16
            )
            dk_h = dot(dscore, query)
            dv_h = dot(prob.astype(jnp.bfloat16), grad)
            dk = dk_h if dk is None else dk + dk_h
            dv = dv_h if dv is None else dv + dv_h
            dqt[c, k, h] += dot(key_t, dscore)
        return dk * SCALE, dv

    def branch_step(step, carry):
        c, k = step // kv_heads, step % kv_heads
        causal = lax.broadcasted_iota(jnp.int32, (length, length), 0) <= lax.broadcasted_iota(
            jnp.int32, (length, length), 1
        )
        dk, dv = grads(c, k, bk_ref[c, :, kv_cols(k, 0)], bv_ref[c, :, kv_cols(k, 0)], causal)
        kg_ref[c, :, kv_cols(k, 0)] = dk.astype(jnp.bfloat16)
        vg_ref[c, :, kv_cols(k, 0)] = dv.astype(jnp.bfloat16)
        return carry

    def branch_steps(start, stop):
        lax.fori_loop(start, stop, branch_step, 0)

    def forward(chunk):
        for d, j in peers:
            if d // half == chunk:
                gather_copy(d, j).wait_recv()
                forward_copy(d, j).start()

    def forwarded(chunk):
        if chunk == 0:
            local.wait()
        for d in range(chunk * half, (chunk + 1) * half):
            for j in range(n_own):
                forward_copy(d, j).wait_recv()

    def prefix_unit(unit):
        chunk, first, last = units[unit]
        buf = gathered[chunk]

        def prefix_step(step, carry):
            c, k = step % slots, step // slots
            p = pref_ref[c]
            key = buf[p, :, :, pair_cols(k, 0)].reshape(chunk_rows, HD)
            val = buf[p, :, :, pair_cols(k, 1)].reshape(chunk_rows, HD)
            dk, dv = grads(c, k, key, val, None)
            acc[k, c, :, :HD] = dk
            acc[k, c, :, HD:] = dv
            return carry

        lax.fori_loop(first * slots, last * slots, prefix_step, 0)

        def combine(dd, carry):
            for k in range(first, last):
                cols = slice((k - first) * 2 * HD, (k - first + 1) * 2 * HD)
                for side in (0, 1):
                    start = pl.multiple_of((dd * 2 + side) * rows, rows)
                    parts = [acc[k, c, pl.ds(start, rows), :] for c in range(slots)]
                    for p in range(num_pre):
                        total = jnp.zeros_like(parts[0])
                        for c in range(slots):
                            total = total + parts[c] * jnp.where(pref_ref[c] == p, 1.0, 0.0)
                        if side == 0:
                            mine[unit][dd, p, :, cols] = total
                        else:
                            outgoing[unit][dd, p, :, cols] = total.astype(jnp.bfloat16)
            return carry

        lax.fori_loop(0, half, combine, 0)
        sibling_copy(unit).start()

    def sibling_copy(unit):
        return pltpu.make_async_remote_copy(
            src_ref=outgoing[unit],
            dst_ref=incoming[unit],
            send_sem=s_send.at[unit],
            recv_sem=s_recv.at[unit],
            device_id=sibling,
            device_id_type=MESH,
        )

    def reduce_copy(unit, d, j):
        return pltpu.make_async_remote_copy(
            src_ref=presum[unit].at[d % half, pl.ds(flip(own, j) * ppo, ppo)],
            dst_ref=land[unit].at[d % half, own],
            send_sem=r_send.at[unit, d % half, j],
            recv_sem=r_recv.at[unit, d % half, j],
            device_id=device(d, j),
            device_id_type=MESH,
        )

    reduce_copies = [
        (unit, d, j) for unit in range(count) for d, j in peers if d // half == units[unit][0]
    ]

    def send_sums(unit):
        sibling_copy(unit).wait_recv()

        def add(dd, carry):
            for p in range(num_pre):
                presum[unit][dd, p] = (
                    mine[unit][dd, p] + incoming[unit][dd, p].astype(jnp.float32)
                ).astype(jnp.bfloat16)
            return carry

        lax.fori_loop(0, half, add, 0)
        for u, d, j in reversed(reduce_copies):
            if u == unit:
                reduce_copy(u, d, j).start()
        if unit == 0:
            land[0][0, own] = presum[0][0, pl.ds(own * ppo, ppo)]

    steps = slots * kv_heads
    early, late = steps * 3 // 8, steps - kv_heads
    branch_steps(0, early)
    forward(0)
    forwarded(0)
    prefix_unit(0)
    branch_steps(early, late)
    send_sums(0)
    forward(1)
    forwarded(1)
    for unit in range(1, count):
        prefix_unit(unit)
        branch_steps(late + unit - 1, late + unit)
        send_sums(unit)

    def finish(step, carry):
        c, k = step // kv_heads, step % kv_heads
        for h in range(GROUPS):
            qg_ref[c, :, head_cols(k, h)] = (dqt[c, k, h] * SCALE).T.astype(jnp.bfloat16)
        return carry

    lax.fori_loop(0, steps, finish, 0)

    for u, d, j in reduce_copies:
        reduce_copy(u, d, j).wait_recv()
    for unit in range(1, count):
        _, first, last = units[unit]
        for k in range(first, last):
            far = slice((k - first) * 2 * HD, (k - first + 1) * 2 * HD)
            near = slice(k * 2 * HD, (k + 1) * 2 * HD)
            for o in range(n_own):
                for i in range(ppo):
                    total = jnp.zeros((rows, 2 * HD), jnp.float32)
                    for d in range(half):
                        total = total + land[0][d, o, i, :, near].astype(jnp.float32)
                        total = total + land[unit][d, o, i, :, far].astype(jnp.float32)
                    start = o * cw + k * HD
                    pk_ref[i, :, start : start + HD] = total[:, :HD].astype(jnp.bfloat16)
                    pv_ref[i, :, start : start + HD] = total[:, HD:].astype(jnp.bfloat16)

    forward_copy(0, 0).wait_send()
    for d, j in peers:
        gather_copy(d, j).wait_send()
        forward_copy(d, j).wait_send()
    for u, d, j in reduce_copies:
        reduce_copy(u, d, j).wait_send()
    for unit in range(count):
        sibling_copy(unit).wait_send()


def per_device(
    queries,
    branch_keys,
    branch_values,
    attn_out,
    out_grad,
    logsumexp,
    prefix_keys,
    prefix_values,
    prefix_of,
    counts,
    *,
    n_own,
    n_br,
):
    slots, length, _ = queries.shape
    cw = branch_keys.shape[2]
    kv_heads = cw // HD
    rows, ppo, full = prefix_keys.shape
    num_pre = n_own * ppo
    planes = n_br // 2
    half = planes // 2

    bf16, f32 = jnp.bfloat16, jnp.float32
    vmem = pl.BlockSpec(memory_space=pltpu.VMEM)
    smem = pl.BlockSpec(memory_space=pltpu.SMEM)
    hbm = pl.BlockSpec(memory_space=pl.ANY)
    dma = pltpu.SemaphoreType.DMA
    widths = [2 * cw] + [2 * HD] * kv_heads
    parts = [(half, num_pre, rows, width) for width in widths]
    lands = [(half, n_own, ppo, rows, width) for width in widths]
    query_grad, key_grad, value_grad, pk, pv = pl.pallas_call(
        functools.partial(kernel, n_own, planes),
        out_shape=(
            jax.ShapeDtypeStruct(queries.shape, bf16),
            jax.ShapeDtypeStruct(branch_keys.shape, bf16),
            jax.ShapeDtypeStruct(branch_keys.shape, bf16),
            jax.ShapeDtypeStruct((ppo, rows, full), bf16),
            jax.ShapeDtypeStruct((ppo, rows, full), bf16),
        ),
        in_specs=[smem, smem, vmem, vmem, vmem] + [hbm] * 5,
        out_specs=(vmem,) * 5,
        scratch_shapes=[
            pltpu.VMEM(queries.shape, bf16),
            pltpu.VMEM(branch_keys.shape, bf16),
            pltpu.VMEM(branch_keys.shape, bf16),
            pltpu.VMEM(queries.shape, bf16),
            pltpu.VMEM(queries.shape, bf16),
            pltpu.VMEM((n_own, ppo, rows, 2 * cw), bf16),
            pltpu.VMEM((num_pre, planes, rows, 2 * cw), bf16),
            pltpu.VMEM((num_pre, planes, rows, 2 * cw), bf16),
            pltpu.VMEM((slots, kv_heads, GROUPS, HD, length), f32),
            pltpu.VMEM((slots, kv_heads, GROUPS, length), f32),
            pltpu.VMEM((slots, kv_heads, GROUPS, length), f32),
            pltpu.VMEM((kv_heads, slots, planes * rows, 2 * HD), f32),
        ]
        + [pltpu.VMEM(part, f32) for part in parts]
        + [pltpu.VMEM(part, bf16) for part in parts] * 3
        + [pltpu.VMEM(block, bf16) for block in lands]
        + [
            dma((5,)),
            dma((planes, n_own)),
            dma((planes, n_own)),
            dma((planes, n_own)),
            dma((planes, n_own)),
            dma(()),
            dma((len(widths),)),
            dma((len(widths),)),
            dma((len(widths), half, n_own)),
            dma((len(widths), half, n_own)),
        ],
        compiler_params=pltpu.CompilerParams(
            collective_id=0, has_side_effects=True, vmem_limit_bytes=56 * 1024 * 1024
        ),
    )(
        prefix_of,
        counts,
        prefix_keys.transpose(1, 0, 2),
        prefix_values.transpose(1, 0, 2),
        logsumexp,
        queries,
        branch_keys,
        branch_values,
        attn_out,
        out_grad,
    )
    return (
        query_grad,
        key_grad,
        value_grad,
        pk.transpose(1, 0, 2),
        pv.transpose(1, 0, 2),
    )


def solution(mesh):
    placed = (
        P("br", None, "own"),
        P("br", None, "own"),
        P("br", None, "own"),
        P("br", None, "own"),
        P("br", None, "own"),
        P("br", "own", None),
        P("br", "own", None),
        P("br", "own", None),
        P("br"),
        P("br"),
    )
    return jax.shard_map(
        functools.partial(per_device, n_own=mesh.shape["own"], n_br=mesh.shape["br"]),
        mesh=mesh,
        in_specs=placed,
        out_specs=(
            P("br", None, "own"),
            P("br", None, "own"),
            P("br", None, "own"),
            P("br", "own", None),
            P("br", "own", None),
        ),
        check_vma=False,
    )
```

time: 92.3 us -> 78.1 us (0.85)
  Pallas kernels: 79.8 us -> 68.8 us
  other arithmetic: 2.89 us -> 0 us
    pallas_call x1, Pallas kernels: 79.8 us -> 68.8 us  [per_device(): pl.pallas_call(functools.partial(kernel, n_own, planes), out_shape=(jax.S...]
    reshape x2 -> x0, local copies, waits for them, and re-layouts: 1.63 us -> none  [the longest x1 0.98 us: per_device(): prefix_values.reshape(rows, ppo, n_own, cw)]
    unnamed x13 -> x14, local copies, waits for them, and re-layouts: 6.41 us -> 7.83 us
    convert_element_type x1 -> x0, other arithmetic: 1.3 us -> none  [per_device(): (prefix_of[:, None] == jnp.arange(num_pre)[None, :]).astype(jnp.float32)]
where the time goes in v2:
time: 78.1 us; the launch traced here: 77.9 us
  Pallas kernels  68.8 us (88%)
  local copies, waits for them, and re-layouts  7.83 us (10%)
  between operations  1.32 us (2%)
    pallas_call x1, Pallas kernels, per_device(): pl.pallas_call(functools.partial(kernel, n_own, planes), out_shape=(jax.S...  68.8 us
    unnamed x14, local copies, waits for them, and re-layouts  7.83 us

profile of v2, /device:TPU:0, one launch (start us, length us, event | category | flops | bytes accessed | tf_op | source)
XLA Modules:
  0.0 77.9 jit_solution(4666487623798937774)
XLA Ops:
  1.3 1.4 %copy.15.lse_ref = f32[4,10,256]{2,1,0:T(8,128)} copy(f32[4,10,256]{2,0,1:T(4,128)} %param.15) | data formatting | bytes 81920 | tf_op args[5]
  2.7 68.8 %shard_map.137 = (bf16[4,256,1280]{2,1,0:T(8,128)(2,1)}, bf16[4,256,256]{2,1,0:T(8,128)(2,1)}, bf16[4,256,256]{2,1,0:T(8,128)(2,1)}, bf16[1,64,1024]{2,1,0:T(8,128)(2,1)}, bf16[1,64,1024]{2,1,0:T(8,128)(2,1)}) custom-call(s32[4]{0:T(128)} %pref_ref.1, s32[1]{0:T(128)S(6)} %copy.21.count_ref, bf16[1,64,1024]{2,1,0:T(8,128)(2,1)} %bitcast.4, ...), custom_call_target="tpu_custom_call" | custom-call | tf_op jit(solution)/shard_map/pallas_call | solution.py:397
  71.5 0.0 copy-start.1
  71.5 0.0 copy-start
  71.5 0.0 copy-start.3
  71.5 0.0 copy-start.2
  71.5 3.5 %copy.22 = bf16[4,256,1280]{2,1,0:T(8,128)(2,1)} copy(bf16[4,256,1280]{2,1,0:T(8,128)(2,1)} %get-tuple-element.20) | data formatting | bytes 5242880
  75.0 0.0 copy-done.1
  75.0 0.8 %copy.23 = bf16[4,256,256]{2,1,0:T(8,128)(2,1)} copy(bf16[4,256,256]{2,1,0:T(8,128)(2,1)S(1)} %copy-done.1) | data formatting | bytes 1048576
  75.8 0.0 copy-done
  75.8 0.8 %copy.24 = bf16[4,256,256]{2,1,0:T(8,128)(2,1)} copy(bf16[4,256,256]{2,1,0:T(8,128)(2,1)S(1)} %copy-done) | data formatting | bytes 1048576
  76.6 0.0 copy-done.3
  76.6 0.7 copy.25
  77.3 0.0 copy-done.2
  77.3 0.7 copy.26
Async XLA Ops:
  71.5 3.5 %copy-start.1 = (bf16[4,256,256]{2,1,0:T(8,128)(2,1)S(1)}, bf16[4,256,256]{2,1,0:T(8,128)(2,1)}, u32[]{:S(2)}) copy-start(bf16[4,256,256]{2,1,0:T(8,128)(2,1)} %get-tuple-element.21) | copy-start | bytes 1572868
  71.5 4.3 %copy-start = (bf16[4,256,256]{2,1,0:T(8,128)(2,1)S(1)}, bf16[4,256,256]{2,1,0:T(8,128)(2,1)}, u32[]{:S(2)}) copy-start(bf16[4,256,256]{2,1,0:T(8,128)(2,1)} %get-tuple-element.22) | copy-start | bytes 1572868
  71.5 5.1 %copy-start.3 = (bf16[1,64,1024]{2,1,0:T(8,128)(2,1)S(1)}, bf16[1,64,1024]{2,1,0:T(8,128)(2,1)}, u32[]{:S(2)}) copy-start(bf16[1,64,1024]{2,1,0:T(8,128)(2,1)} %get-tuple-element.13) | copy-start | bytes 393220
  71.5 5.8 %copy-start.2 = (bf16[1,64,1024]{2,1,0:T(8,128)(2,1)S(1)}, bf16[1,64,1024]{2,1,0:T(8,128)(2,1)}, u32[]{:S(2)}) copy-start(bf16[1,64,1024]{2,1,0:T(8,128)(2,1)} %get-tuple-element.14) | copy-start | bytes 393220

commit v3 on v2

--- a/solution.py
+++ b/solution.py
@@ -48,11 +48,14 @@
     bv_hbm,
     ao_hbm,
     og_hbm,
+    qg_hbm,
+    kg_hbm,
+    vg_hbm,
+    pk_ref,
+    pv_ref,
     qg_ref,
     kg_ref,
     vg_ref,
-    pk_ref,
-    pv_ref,
     q_ref,
     bk_ref,
     bv_ref,
@@ -80,8 +83,8 @@
     gathered = (g0, g1)
     units = [(0, 0, kv_heads)] + [(1, k, k + 1) for k in range(kv_heads)]
     count = len(units)
-    mine, outgoing, incoming, presum, land = (
-        rest[i * count : (i + 1) * count] for i in range(5)
+    mine, outgoing, incoming, presum, land, hops, total_b = (
+        rest[i * count : (i + 1) * count] for i in range(7)
     )
     (
         load_sem,
@@ -94,13 +97,17 @@
         s_recv,
         r_send,
         r_recv,
-    ) = rest[5 * count :]
+        h_send,
+        h_recv,
+        store_sem,
+    ) = rest[7 * count :]
 
     def device(d, j):
         return {"own": flip(own, j), "br": flip(plane, d) * 2 + core}
 
     sibling = {"own": own, "br": plane * 2 + 1 - core}
-    peers = [(d, j) for d in range(planes) for j in range(n_own) if (d, j) != (0, 0)]
+    blocks = [(d, j) for d in range(planes) for j in range(n_own) if (d, j) != (0, 0)]
+    peers = [(d, j) for d, j in blocks if d <= half]
 
     barrier = pltpu.get_barrier_semaphore()
     for d, j in peers:
@@ -137,12 +144,14 @@
         return gathered[d // half].at[pl.ds(o * ppo, ppo), 2 * (d % half) + side]
 
     def gather_copy(d, j):
+        o = flip(own, j)
+        relay = d > half
         return pltpu.make_async_remote_copy(
-            src_ref=src.at[flip(own, j)],
-            dst_ref=place(d, own, 0),
+            src_ref=place(half, o, 0) if relay else src.at[o],
+            dst_ref=place(d, o if relay else own, 0),
             send_sem=g_send.at[d, j],
             recv_sem=g_recv.at[d, j],
-            device_id=device(d, j),
+            device_id=device(d - half, 0) if relay else device(d, j),
             device_id_type=MESH,
         )
 
@@ -182,7 +191,7 @@
             grad = og_ref[c, :, head_cols(k, h)].astype(jnp.float32)
             product = grad * ao_ref[c, :, head_cols(k, h)].astype(jnp.float32)
             delta[c, k, pl.ds(h, 1), :] = jnp.sum(product.T, axis=0, keepdims=True)
-            lse2[c, k, pl.ds(h, 1), :] = lse_ref[c, pl.ds(k * GROUPS + h, 1), :] * LOG2E + dead
+            lse2[c, k, pl.ds(h, 1), :] = lse_ref[k * GROUPS + h, pl.ds(c, 1), :] * LOG2E + dead
             dqt[c, k, h] = jnp.zeros((HD, length), jnp.float32)
         return carry
 
@@ -224,10 +233,13 @@
     def branch_steps(start, stop):
         lax.fori_loop(start, stop, branch_step, 0)
 
-    def forward(chunk):
-        for d, j in peers:
-            if d // half == chunk:
+    def forward(first, last):
+        for d, j in blocks:
+            if first <= d < last:
                 gather_copy(d, j).wait_recv()
+                if d == half:
+                    for e in range(1, half):
+                        gather_copy(half + e, j).start()
                 forward_copy(d, j).start()
 
     def forwarded(chunk):
@@ -251,7 +263,11 @@
             acc[k, c, :, HD:] = dv
             return carry
 
-        lax.fori_loop(first * slots, last * slots, prefix_step, 0)
+        lax.fori_loop(first * slots, (first + 1) * slots, prefix_step, 0)
+        if chunk == 0:
+            forward(half, half + 1)
+        if last > first + 1:
+            lax.fori_loop((first + 1) * slots, last * slots, prefix_step, 0)
 
         def combine(dd, carry):
             for k in range(first, last):
@@ -283,50 +299,87 @@
         )
 
     def reduce_copy(unit, d, j):
+        o = flip(own, j)
+        if unit == 0:
+            source, target = presum[0].at[d, pl.ds(o * ppo, ppo)], land[0].at[d, own]
+        else:
+            source, target = total_b[unit].at[pl.ds(o * ppo, ppo)], land[unit].at[0, own]
         return pltpu.make_async_remote_copy(
-            src_ref=presum[unit].at[d % half, pl.ds(flip(own, j) * ppo, ppo)],
-            dst_ref=land[unit].at[d % half, own],
+            src_ref=source,
+            dst_ref=target,
             send_sem=r_send.at[unit, d % half, j],
             recv_sem=r_recv.at[unit, d % half, j],
             device_id=device(d, j),
             device_id_type=MESH,
         )
 
+    def hop_copy(unit, e):
+        return pltpu.make_async_remote_copy(
+            src_ref=presum[unit].at[e],
+            dst_ref=hops[unit].at[e - 1],
+            send_sem=h_send.at[unit, e],
+            recv_sem=h_recv.at[unit, e],
+            device_id=device(e, 0),
+            device_id_type=MESH,
+        )
+
     reduce_copies = [
         (unit, d, j) for unit in range(count) for d, j in peers if d // half == units[unit][0]
     ]
 
-    def send_sums(unit):
-        sibling_copy(unit).wait_recv()
+    def send_near():
+        sibling_copy(0).wait_recv()
 
         def add(dd, carry):
             for p in range(num_pre):
-                presum[unit][dd, p] = (
-                    mine[unit][dd, p] + incoming[unit][dd, p].astype(jnp.float32)
+                presum[0][dd, p] = (
+                    mine[0][dd, p] + incoming[0][dd, p].astype(jnp.float32)
                 ).astype(jnp.bfloat16)
             return carry
 
         lax.fori_loop(0, half, add, 0)
         for u, d, j in reversed(reduce_copies):
+            if u == 0:
+                reduce_copy(u, d, j).start()
+        land[0][0, own] = presum[0][0, pl.ds(own * ppo, ppo)]
+
+    def send_hops(unit):
+        sibling_copy(unit).wait_recv()
+        for e in range(1, half):
+            for p in range(num_pre):
+                presum[unit][e, p] = (
+                    mine[unit][e, p] + incoming[unit][e, p].astype(jnp.float32)
+                ).astype(jnp.bfloat16)
+            hop_copy(unit, e).start()
+
+    def send_far(unit):
+        for e in range(1, half):
+            hop_copy(unit, e).wait_recv()
+        for p in range(num_pre):
+            total = mine[unit][0, p] + incoming[unit][0, p].astype(jnp.float32)
+            for e in range(1, half):
+                total = total + hops[unit][e - 1, p].astype(jnp.float32)
+            total_b[unit][p] = total.astype(jnp.bfloat16)
+        for u, d, j in reduce_copies:
             if u == unit:
                 reduce_copy(u, d, j).start()
-        if unit == 0:
-            land[0][0, own] = presum[0][0, pl.ds(own * ppo, ppo)]
 
     steps = slots * kv_heads
     early, late = steps * 3 // 8, steps - kv_heads
     branch_steps(0, early)
-    forward(0)
+    forward(0, half)
     forwarded(0)
     prefix_unit(0)
     branch_steps(early, late)
-    send_sums(0)
-    forward(1)
+    send_near()
+    forward(half + 1, planes)
     forwarded(1)
     for unit in range(1, count):
         prefix_unit(unit)
+        if unit > 1:
+            send_far(unit - 1)
         branch_steps(late + unit - 1, late + unit)
-        send_sums(unit)
+        send_hops(unit)
 
     def finish(step, carry):
         c, k = step // kv_heads, step % kv_heads
@@ -335,6 +388,13 @@
         return carry
 
     lax.fori_loop(0, steps, finish, 0)
+    stores = [
+        pltpu.make_async_copy(ref, out, store_sem.at[i])
+        for i, (ref, out) in enumerate(((qg_ref, qg_hbm), (kg_ref, kg_hbm), (vg_ref, vg_hbm)))
+    ]
+    for store in stores:
+        store.start()
+    send_far(count - 1)
 
     for u, d, j in reduce_copies:
         reduce_copy(u, d, j).wait_recv()
@@ -348,19 +408,53 @@
                     total = jnp.zeros((rows, 2 * HD), jnp.float32)
                     for d in range(half):
                         total = total + land[0][d, o, i, :, near].astype(jnp.float32)
-                        total = total + land[unit][d, o, i, :, far].astype(jnp.float32)
+                    total = total + land[unit][0, o, i, :, far].astype(jnp.float32)
                     start = o * cw + k * HD
                     pk_ref[i, :, start : start + HD] = total[:, :HD].astype(jnp.bfloat16)
                     pv_ref[i, :, start : start + HD] = total[:, HD:].astype(jnp.bfloat16)
 
     forward_copy(0, 0).wait_send()
-    for d, j in peers:
+    for d, j in blocks:
         gather_copy(d, j).wait_send()
         forward_copy(d, j).wait_send()
+    for unit in range(1, count):
+        for e in range(1, half):
+            hop_copy(unit, e).wait_send()
+    for store in stores:
+        store.wait()
     for u, d, j in reduce_copies:
         reduce_copy(u, d, j).wait_send()
     for unit in range(count):
         sibling_copy(unit).wait_send()
+
+
+def copy_kernel(*refs):
+    count = (len(refs) - 1) // 2
+    sems = refs[-1]
+    copies = []
+    for source, target in zip(refs[:count], refs[count : 2 * count]):
+        pieces = source.shape[0] if len(source.shape) == 3 else 1
+        for i in range(pieces):
+            copies.append(
+                pltpu.make_async_copy(source.at[i], target.at[i], sems.at[len(copies)])
+            )
+    for copy in copies:
+        copy.start()
+    for copy in copies:
+        copy.wait()
+
+
+def write_out(arrays):
+    any_spec = pl.BlockSpec(memory_space=pl.ANY)
+    pieces = sum(array.shape[0] for array in arrays)
+    return pl.pallas_call(
+        copy_kernel,
+        out_shape=tuple(jax.ShapeDtypeStruct(a.shape, a.dtype) for a in arrays),
+        in_specs=[any_spec] * len(arrays),
+        out_specs=(any_spec,) * len(arrays),
+        scratch_shapes=[pltpu.SemaphoreType.DMA((pieces,))],
+        compiler_params=pltpu.CompilerParams(vmem_limit_bytes=60 * 1024 * 1024),
+    )(*arrays)
 
 
 def per_device(
@@ -393,8 +487,12 @@
     dma = pltpu.SemaphoreType.DMA
     widths = [2 * cw] + [2 * HD] * kv_heads
     parts = [(half, num_pre, rows, width) for width in widths]
-    lands = [(half, n_own, ppo, rows, width) for width in widths]
-    query_grad, key_grad, value_grad, pk, pv = pl.pallas_call(
+    lands = [
+        (half if unit == 0 else 1, n_own, ppo, rows, width) for unit, width in enumerate(widths)
+    ]
+    hops = [(max(half - 1, 1), num_pre, rows, width) for width in widths]
+    totals = [(num_pre, rows, width) for width in widths]
+    grads = pl.pallas_call(
         functools.partial(kernel, n_own, planes),
         out_shape=(
             jax.ShapeDtypeStruct(queries.shape, bf16),
@@ -404,8 +502,11 @@
             jax.ShapeDtypeStruct((ppo, rows, full), bf16),
         ),
         in_specs=[smem, smem, vmem, vmem, vmem] + [hbm] * 5,
-        out_specs=(vmem,) * 5,
+        out_specs=(hbm,) * 3 + (vmem,) * 2,
         scratch_shapes=[
+            pltpu.VMEM(queries.shape, bf16),
+            pltpu.VMEM(branch_keys.shape, bf16),
+            pltpu.VMEM(branch_keys.shape, bf16),
             pltpu.VMEM(queries.shape, bf16),
             pltpu.VMEM(branch_keys.shape, bf16),
             pltpu.VMEM(branch_keys.shape, bf16),
@@ -421,7 +522,7 @@
         ]
         + [pltpu.VMEM(part, f32) for part in parts]
         + [pltpu.VMEM(part, bf16) for part in parts] * 3
-        + [pltpu.VMEM(block, bf16) for block in lands]
+        + [pltpu.VMEM(block, bf16) for block in lands + hops + totals]
         + [
             dma((5,)),
             dma((planes, n_own)),
@@ -433,6 +534,9 @@
             dma((len(widths),)),
             dma((len(widths), half, n_own)),
             dma((len(widths), half, n_own)),
+            dma((len(widths), half)),
+            dma((len(widths), half)),
+            dma((3,)),
         ],
         compiler_params=pltpu.CompilerParams(
             collective_id=0, has_side_effects=True, vmem_limit_bytes=56 * 1024 * 1024
@@ -442,13 +546,14 @@
         counts,
         prefix_keys.transpose(1, 0, 2),
         prefix_values.transpose(1, 0, 2),
-        logsumexp,
+        logsumexp.transpose(1, 0, 2),
         queries,
         branch_keys,
         branch_values,
         attn_out,
         out_grad,
     )
+    query_grad, key_grad, value_grad, pk, pv = write_out(grads)
     return (
         query_grad,
         key_grad,

time: 78.1 us -> 191 us (2.45)
  Pallas kernels: 68.8 us -> 190 us
  local copies, waits for them, and re-layouts: 7.83 us -> 0 us
    pallas_call x0 -> x1, Pallas kernels: none -> 120 us  [write_out(): pl.pallas_call(copy_kernel, out_shape=tuple((jax.ShapeDtypeStruct(a.shape...]
    unnamed x14 -> x0, local copies, waits for them, and re-layouts: 7.83 us -> none
where the time goes in v3:
time: 191 us
  Pallas kernels  190 us (99%)
    pallas_call x1, Pallas kernels, write_out(): pl.pallas_call(copy_kernel, out_shape=tuple((jax.ShapeDtypeStruct(a.shape...  120 us
    pallas_call x1, Pallas kernels, per_device(): pl.pallas_call(functools.partial(kernel, n_own, planes), out_shape=(jax.S...  69.7 us

profile of v3, /device:TPU:0, one launch (start us, length us, event | category | flops | bytes accessed | tf_op | source)
XLA Modules:
  0.0 191.3 jit_solution(5900626948421232380)
XLA Ops:
  1.3 69.7 %shard_map.137 = (bf16[4,256,1280]{2,1,0:T(8,128)(2,1)}, bf16[4,256,256]{2,1,0:T(8,128)(2,1)}, bf16[4,256,256]{2,1,0:T(8,128)(2,1)}, bf16[1,64,1024]{2,1,0:T(8,128)(2,1)}, bf16[1,64,1024]{2,1,0:T(8,128)(2,1)}) custom-call(s32[4]{0:T(128)} %pref_ref.1, s32[1]{0:T(128)S(6)} %copy.15.count_ref, bf16[1,64,1024]{2,1,0:T(8,128)(2,1)} %bitcast.5, ...), custom_call_target="tpu_custom_call" | custom-call | tf_op jit(solution)/shard_map/pallas_call | solution.py:495
  71.0 120.3 %shard_map.138 = (bf16[4,256,1280]{2,1,0:T(8,128)(2,1)}, bf16[4,256,256]{2,1,0:T(8,128)(2,1)}, bf16[4,256,256]{2,1,0:T(8,128)(2,1)}, bf16[1,64,1024]{2,1,0:T(8,128)(2,1)}, bf16[1,64,1024]{2,1,0:T(8,128)(2,1)}) custom-call(bf16[4,256,1280]{2,1,0:T(8,128)(2,1)} %get-tuple-element.15.refs_0_, bf16[4,256,256]{2,1,0:T(8,128)(2,1)} %get-tuple-element.16.refs_1_, ...), custom_call_target="tpu_custom_call" | custom-call | tf_op jit(solution)/shard_map/pallas_call | solution.py:450

commit v4 on v3

--- a/solution.py
+++ b/solution.py
@@ -429,19 +429,23 @@
 
 
 def copy_kernel(*refs):
-    count = (len(refs) - 1) // 2
-    sems = refs[-1]
-    copies = []
-    for source, target in zip(refs[:count], refs[count : 2 * count]):
-        pieces = source.shape[0] if len(source.shape) == 3 else 1
-        for i in range(pieces):
-            copies.append(
-                pltpu.make_async_copy(source.at[i], target.at[i], sems.at[len(copies)])
-            )
-    for copy in copies:
-        copy.start()
-    for copy in copies:
-        copy.wait()
+    count = (len(refs) - 2) // 3
+    read_sems, write_sems = refs[-2:]
+    reads, writes = [], []
+    for source, target, held in zip(
+        refs[:count], refs[count : 2 * count], refs[2 * count : 3 * count]
+    ):
+        for i in range(source.shape[0]):
+            n = len(reads)
+            reads.append(pltpu.make_async_copy(source.at[i], held.at[i], read_sems.at[n]))
+            writes.append(pltpu.make_async_copy(held.at[i], target.at[i], write_sems.at[n]))
+    for read in reads:
+        read.start()
+    for read, write in zip(reads, writes):
+        read.wait()
+        write.start()
+    for write in writes:
+        write.wait()
 
 
 def write_out(arrays):
@@ -452,7 +456,8 @@
         out_shape=tuple(jax.ShapeDtypeStruct(a.shape, a.dtype) for a in arrays),
         in_specs=[any_spec] * len(arrays),
         out_specs=(any_spec,) * len(arrays),
-        scratch_shapes=[pltpu.SemaphoreType.DMA((pieces,))],
+        scratch_shapes=[pltpu.VMEM(a.shape, a.dtype) for a in arrays]
+        + [pltpu.SemaphoreType.DMA((pieces,))] * 2,
         compiler_params=pltpu.CompilerParams(vmem_limit_bytes=60 * 1024 * 1024),
     )(*arrays)
 

time: 191 us -> 74.4 us (0.39)
  Pallas kernels: 190 us -> 72.9 us
    pallas_call x1, Pallas kernels: 120 us -> 3.24 us  [write_out(): pl.pallas_call(copy_kernel, out_shape=tuple((jax.ShapeDtypeStruct(a.shape...]
where the time goes in v4:
time: 74.4 us; the launch traced here: 74.2 us
  Pallas kernels  72.9 us (98%)
  between operations  1.29 us (2%)
    pallas_call x1, Pallas kernels, per_device(): pl.pallas_call(functools.partial(kernel, n_own, planes), out_shape=(jax.S...  69.7 us
    pallas_call x1, Pallas kernels, write_out(): pl.pallas_call(copy_kernel, out_shape=tuple((jax.ShapeDtypeStruct(a.shape...  3.24 us

profile of v4, /device:TPU:0, one launch (start us, length us, event | category | flops | bytes accessed | tf_op | source)
XLA Modules:
  0.0 74.2 jit_solution(3393967506471121435)
XLA Ops:
  1.3 69.7 %shard_map.137 = (bf16[4,256,1280]{2,1,0:T(8,128)(2,1)}, bf16[4,256,256]{2,1,0:T(8,128)(2,1)}, bf16[4,256,256]{2,1,0:T(8,128)(2,1)}, bf16[1,64,1024]{2,1,0:T(8,128)(2,1)}, bf16[1,64,1024]{2,1,0:T(8,128)(2,1)}) custom-call(s32[4]{0:T(128)} %pref_ref.1, s32[1]{0:T(128)S(6)} %copy.15.count_ref, bf16[1,64,1024]{2,1,0:T(8,128)(2,1)} %bitcast.5, ...), custom_call_target="tpu_custom_call" | custom-call | tf_op jit(solution)/shard_map/pallas_call | solution.py:500
  71.0 3.2 %shard_map.138 = (bf16[4,256,1280]{2,1,0:T(8,128)(2,1)}, bf16[4,256,256]{2,1,0:T(8,128)(2,1)}, bf16[4,256,256]{2,1,0:T(8,128)(2,1)}, bf16[1,64,1024]{2,1,0:T(8,128)(2,1)}, bf16[1,64,1024]{2,1,0:T(8,128)(2,1)}) custom-call(bf16[4,256,1280]{2,1,0:T(8,128)(2,1)} %get-tuple-element.15.refs_0_, bf16[4,256,256]{2,1,0:T(8,128)(2,1)} %get-tuple-element.16.refs_1_, ...), custom_call_target="tpu_custom_call" | custom-call | tf_op jit(solution)/shard_map/pallas_call | solution.py:454
